TPU v7x, 256 devices: a whole 4x4x8 slice. The times are simulated.
256 devices in a mesh: rep: 4 (over y), exp: 64 (over z, x, core).
Axes of the slice: x: 4, y: 4, z: 8, core: 2. Of those that a mesh axis runs over, the one named last changes fastest.
Arguments:
- tokens: bfloat16 [32768, 1024], P(('rep', 'exp')), may hold values from -6 to 6
- gain: float32 [1024], replicated, may hold values from 0.1 to 1.9
- expert_ids: int32 [32768, 2], P(('rep', 'exp')), may hold values from 0 to 63, all different within a row
- gates: float32 [32768, 2], P(('rep', 'exp')), may hold values from 0.1 to 0.9
- w_in: bfloat16 [64, 1024, 4096], P('exp', None, 'rep'), may hold values from -0.1875 to 0.1875
- w_out: bfloat16 [64, 4096, 1024], P('exp', 'rep'), may hold values from -0.09375 to 0.09375
- cotangent: bfloat16 [32768, 1024], P(('rep', 'exp')), may hold values from -6 to 6
Outputs:
- mixed: bfloat16 [32768, 1024], P(('rep', 'exp'))
- grad_tokens: bfloat16 [32768, 1024], P(('rep', 'exp'))
- grad_in: bfloat16 [64, 1024, 4096], P('exp', None, 'rep')
- grad_out: bfloat16 [64, 4096, 1024], P('exp', 'rep')
Inputs may be any that keep to these rules, and one draw needn't show every extreme that they name: `expert_ids`: each token names two different experts, and every expert is named by some token.
All inputs are finite; a program needn't handle non-finite values.
Results may differ from a plain program's by a relative error of at most 0.007.
Values may be sent and summed in bfloat16 or wider, within the bound.
A program may use at most 64 MiB of HBM per device.

v0:
```python
import jax
import jax.numpy as jnp
from jax import lax
from jax.sharding import PartitionSpec as P

epsilon = 1e-05


def normalize(entries, gain):
    center = entries - jnp.mean(entries, axis=-1, keepdims=True)
    spread = jnp.mean(center * center, axis=-1, keepdims=True)
    return center * lax.rsqrt(spread + epsilon) * gain


def activate(entries):
    return jax.nn.gelu(entries, approximate=True)


def slot_table(expert_ids, experts, capacity):
    flattened = expert_ids.reshape(-1)
    labels = jnp.arange(experts, dtype=jnp.int32)
    onehot = (flattened[:, None] == labels[None, :]).astype(jnp.int32)
    before = jnp.cumsum(onehot, axis=0) - onehot
    ranking = jnp.sum(before * onehot, axis=1)
    target = jnp.where(ranking < capacity, flattened * capacity + ranking, -1)
    places = jnp.arange(experts * capacity, dtype=jnp.int32)
    return (target[None, :] == places[:, None]).astype(jnp.bfloat16)


def place_rows(select, paired, experts, capacity):
    packed = jnp.dot(select, paired, preferred_element_type=jnp.float32).astype(jnp.bfloat16)
    return packed.reshape(experts, capacity, paired.shape[1])


def take_rows(select, landed):
    flattened = landed.reshape(-1, landed.shape[-1])
    return jnp.einsum("sp,sd->pd", select, flattened, preferred_element_type=jnp.float32)


def expert_forward(in_rows, w_first):
    preact = jnp.dot(in_rows, w_first, preferred_element_type=jnp.float32)
    activated, act_back = jax.vjp(activate, preact)
    return (activated.astype(jnp.bfloat16), act_back)


def expert_backward(in_rows, hidden, act_back, grad_rows, w_first, w_second):
    d_hidden = jnp.einsum("rd,fd->rf", grad_rows, w_second, preferred_element_type=jnp.float32)
    d_pre = act_back(d_hidden)[0].astype(jnp.bfloat16)
    grad_second = jnp.einsum(
        "rf,rd->fd", hidden, grad_rows, preferred_element_type=jnp.float32
    ).astype(jnp.bfloat16)
    grad_first = jnp.einsum("rd,rf->df", in_rows, d_pre, preferred_element_type=jnp.float32).astype(
        jnp.bfloat16
    )
    partial_value = jnp.einsum("rf,df->rd", d_pre, w_first, preferred_element_type=jnp.float32)
    return (partial_value, grad_first, grad_second)


def arrive(sent):
    landed = lax.all_to_all(sent, "exp", split_axis=0, concat_axis=0, tiled=True)
    return lax.all_gather(landed.reshape(-1, landed.shape[-1]), "rep", axis=0, tiled=True)


def depart(partial_value, experts, capacity):
    summed = lax.psum_scatter(
        partial_value.astype(jnp.bfloat16), "rep", scatter_dimension=0, tiled=True
    )
    return lax.all_to_all(
        summed.reshape(experts, capacity, summed.shape[-1]),
        "exp",
        split_axis=0,
        concat_axis=0,
        tiled=True,
    )


def local(tokens, gain, expert_ids, gates, w_in, w_out, cotangent):
    experts = lax.axis_size("exp")
    tok_count = tokens.shape[0]
    features = tokens.shape[1]
    capacity = max(2, 2 * tok_count // experts)
    values = tokens.astype(jnp.float32)
    normed, norm_back = jax.vjp(lambda entries: normalize(entries, gain), values)
    normed = normed.astype(jnp.bfloat16)
    select = slot_table(expert_ids, experts, capacity)
    x_sent = place_rows(select, jnp.repeat(normed, 2, axis=0), experts, capacity)
    scaled = (cotangent.astype(jnp.float32)[:, None, :] * gates[:, :, None]).astype(jnp.bfloat16)
    d_sent = place_rows(select, scaled.reshape(2 * tok_count, features), experts, capacity)
    w_first = w_in[0]
    w_second = w_out[0]
    x_rows = arrive(x_sent)
    hidden, act_back = expert_forward(x_rows, w_first)
    y_partial = jnp.dot(hidden, w_second, preferred_element_type=jnp.float32)
    y_back = depart(y_partial, experts, capacity)
    d_rows = arrive(d_sent)
    partial_value, grad_first, grad_second = expert_backward(
        x_rows, hidden, act_back, d_rows, w_first, w_second
    )
    d_back = depart(partial_value, experts, capacity)
    returned = take_rows(select, y_back).reshape(tok_count, 2, features)
    mixed = (values + jnp.sum(gates[:, :, None] * returned, axis=1)).astype(jnp.bfloat16)
    d_normed = jnp.sum(take_rows(select, d_back).reshape(tok_count, 2, features), axis=1)
    grad_tokens = (cotangent.astype(jnp.float32) + norm_back(d_normed)[0]).astype(jnp.bfloat16)
    return (mixed, grad_tokens, grad_first[None], grad_second[None])


def solution(mesh):
    return jax.shard_map(
        local,
        mesh=mesh,
        in_specs=(
            P(("rep", "exp"), None),
            P(),
            P(("rep", "exp"), None),
            P(("rep", "exp"), None),
            P("exp", None, "rep"),
            P("exp", "rep", None),
            P(("rep", "exp"), None),
        ),
        out_specs=(
            P(("rep", "exp"), None),
            P(("rep", "exp"), None),
            P("exp", None, "rep"),
            P("exp", "rep", None),
        ),
        check_vma=False,
    )
```

profile of v0, /device:TPU:1, one launch (start us, length us, event | category | flops | bytes accessed | tf_op | source)
XLA Modules:
  0.0 222.1 jit_solution(7395748226251307991)
XLA Ops:
  7.2 0.9 copy.11
  8.2 0.1 eq.60
  8.3 0.1 eq.64
  8.5 1.1 convert_reduce_fusion
  9.5 1.2 fusion.28
  10.7 0.6 reduce-window.6
  11.4 0.2 slice_reduce_fusion
  11.7 1.2 fusion.30
  12.9 0.3 broadcast_in_dim.32
  13.2 0.2 reshape.119
  13.4 0.3 convolution_convert_fusion.1
  13.7 0.2 reshape.120
  13.9 30.5 %all_to_all.20 = bf16[64,4,1024]{2,1,0:T(4,128)(2,1)S(1)} all-to-all(bf16[64,4,1024]{2,1,0:T(4,128)(2,1)S(1)} %reshape.120), channel_id=1, replica_groups=mesh['rep'=4,'exp'=64] {'exp'}, dimensions={0} | all-to-all | bytes 1048576 | tf_op jit(solution)/shard_map/all_to_all | solution.py:60
  44.4 0.9 reshape.121
  45.4 0.1 copy.17
  45.5 0.1 mul.152
  45.7 0.3 mul.150
  45.9 1.7 mul.151
  47.6 1.6 convolution_convert_fusion
  49.2 0.2 reshape.124
  49.4 23.2 %all_to_all.21 = bf16[64,4,1024]{2,1,0:T(4,128)(2,1)S(1)} all-to-all(bf16[64,4,1024]{2,1,0:T(4,128)(2,1)S(1)} %reshape.124), channel_id=1, replica_groups=mesh['rep'=4,'exp'=64] {'exp'}, dimensions={0} | all-to-all | bytes 1048576 | tf_op jit(solution)/shard_map/all_to_all | solution.py:60
  72.7 0.9 reshape.125
  73.7 1.8 all-gather.3.cloned.1.call-done
  75.4 4.5 %fusion.15 = f32[1024,1024]{1,0:T(8,128)S(1)} fusion(bf16[1024,1024]{1,0:T(8,128)(2,1)} %all-gather.3.cloned.1.call-done, bf16[1,1024,1024]{2,1,0:T(8,128)(2,1)} %param.11), kind=kOutput, calls=%fused_computation.16 | convolution fusion | flops 2147483648 | bytes 8388608 | tf_op jit(solution)/shard_map/dot_general | solution.py:41
  80.0 1.9 copy-done.8
  81.9 4.0 %fusion.20 = bf16[1024,1024]{1,0:T(8,128)(2,1)} fusion(bf16[1,1024,1024]{2,1,0:T(8,128)(2,1)S(1)} %copy-done, f32[1024,1024]{1,0:T(8,128)S(1)} %fusion.15), kind=kOutput, calls=%fused_computation.21 | convolution fusion | flops 2157969408 | bytes 8388608 | tf_op jit(solution)/shard_map/dot_general | solution.py:93
  85.9 0.2 reduce-scatter.5.cloned.1.call-start
  86.2 25.1 %all-gather.5.cloned.1.call-done = bf16[1024,1024]{1,0:T(8,128)(2,1)} async-done(((bf16[256,1024]{1,0:T(8,128)(2,1)}), bf16[1024,1024]{1,0:T(8,128)(2,1)}) %all-gather.5.cloned.1.call-update) | async-done | bytes 2097168 | tf_op jit(solution)/shard_map/all_gather | solution.py:61
  111.3 7.2 %fusion.6 = bf16[1024,1024]{1,0:T(8,128)(2,1)S(1)} fusion(f32[1024,1024]{1,0:T(8,128)} %copy-done.8, bf16[1024,1024]{1,0:T(8,128)(2,1)} %all-gather.5.cloned.1.call-done, bf16[1,1024,1024]{2,1,0:T(8,128)(2,1)S(1)} %copy-done), kind=kOutput, calls=%fused_computation.8 | convolution fusion | flops 2168455168 | bytes 10485760 | tf_op jit(solution)/shard_map/rd,fd->rf/dot_general | solution.py:47
  118.5 1.4 copy-done.10
  119.9 3.7 %fusion.17 = bf16[1024,1024]{1,0:T(8,128)(2,1)} fusion(bf16[1024,1024]{1,0:T(8,128)(2,1)S(1)} %fusion.6, bf16[1,1024,1024]{2,1,0:T(8,128)(2,1)S(1)} %copy-done.6), kind=kOutput, calls=%fused_computation.20 | convolution fusion | flops 2148532224 | bytes 6291456 | tf_op jit(solution)/shard_map/rf,df->rd/dot_general | solution.py:55
  123.6 23.2 %reduce-scatter.3.cloned.1.call-done = bf16[256,1024]{1,0:T(8,128)(2,1)} async-done(((bf16[1024,1024]{1,0:T(8,128)(2,1)}), bf16[256,1024]{1,0:T(8,128)(2,1)}) %reduce-scatter.3.cloned.1.call-update) | async-done | bytes 524304 | tf_op jit(solution)/shard_map/reduce_scatter | solution.py:65
  146.8 2.0 reshape.122
  148.8 10.6 %all-to-all-start.1 = ((bf16[64,4,1024]{2,1,0:T(4,128)(2,1)}), bf16[64,4,1024]{2,1,0:T(4,128)(2,1)S(1)}, u32[]{:S(2)}, u32[]{:S(2)}) async-start(bf16[64,4,1024]{2,1,0:T(4,128)(2,1)} %reshape.122), calls=%async_computation.2 | async-start | bytes 1048576 | tf_op jit(solution)/shard_map/all_to_all | solution.py:68
  159.4 0.1 reduce_sum.74
  159.8 22.2 %reduce-scatter.5.cloned.1.call-done = bf16[256,1024]{1,0:T(8,128)(2,1)} async-done(((bf16[1024,1024]{1,0:T(8,128)(2,1)}), bf16[256,1024]{1,0:T(8,128)(2,1)}) %reduce-scatter.5.cloned.1.call-update) | async-done | bytes 524304 | tf_op jit(solution)/shard_map/reduce_scatter | solution.py:65
  182.0 2.1 reshape.126
  184.1 10.6 %all-to-all-start.3 = ((bf16[64,4,1024]{2,1,0:T(4,128)(2,1)}), bf16[64,4,1024]{2,1,0:T(4,128)(2,1)S(1)}, u32[]{:S(2)}, u32[]{:S(2)}) async-start(bf16[64,4,1024]{2,1,0:T(4,128)(2,1)} %reshape.126), calls=%async_computation.5 | async-start | bytes 1048576 | tf_op jit(solution)/shard_map/all_to_all | solution.py:68
  194.7 6.1 %convert_bitcast_fusion.1 = bf16[1,1024,1024]{2,1,0:T(8,128)(2,1)} fusion(bf16[1024,1024]{1,0:T(8,128)(2,1)} %all-gather.3.cloned.1.call-done, bf16[1024,1024]{1,0:T(8,128)(2,1)} %copy-done.10), kind=kOutput, calls=%fused_computation.19 | convolution fusion | flops 2148532224 | bytes 6291456 | tf_op jit(solution)/shard_map/rd,rf->df/dot_general | solution.py:52
  200.8 4.1 %convert_bitcast_fusion = bf16[1,1024,1024]{2,1,0:T(8,128)(2,1)} fusion(bf16[1024,1024]{1,0:T(8,128)(2,1)S(1)} %copy-done.7, f32[1024,1024]{1,0:T(8,128)S(1)} %copy-done.9), kind=kOutput, calls=%fused_computation.18 | convolution fusion | flops 2157969408 | bytes 8388608 | tf_op jit(solution)/shard_map/rf,rd->fd/dot_general | solution.py:49
  204.9 0.9 reshape.128
  205.8 2.2 fusion.23
  208.0 4.4 %all-to-all-done.3 = bf16[64,4,1024]{2,1,0:T(4,128)(2,1)S(1)} async-done(((bf16[64,4,1024]{2,1,0:T(4,128)(2,1)}), bf16[64,4,1024]{2,1,0:T(4,128)(2,1)S(1)}, u32[]{:S(2)}, u32[]{:S(2)}) %all-to-all-start.3) | async-done | bytes 524320 | tf_op jit(solution)/shard_map/all_to_all | solution.py:68
  212.4 0.1 reshape.129
  212.5 0.3 convolution_reduce_fusion
  212.9 0.2 fusion.31
  213.1 0.3 fusion.46
  213.4 2.1 add_convert_fusion
  (41 shorter events, 0.6 us)
Async XLA Ops:
  7.2 74.8 %copy-start = (bf16[1,1024,1024]{2,1,0:T(8,128)(2,1)S(1)}, bf16[1,1024,1024]{2,1,0:T(8,128)(2,1)}, u32[]{:S(2)}) copy-start(bf16[1,1024,1024]{2,1,0:T(8,128)(2,1)} %param.12) | copy-start | bytes 6291460
  7.2 38.2 %copy-start.5 = (f32[128,2]{0,1:T(2,128)S(1)}, f32[128,2]{0,1:T(2,128)}, u32[]{:S(2)}) copy-start(f32[128,2]{0,1:T(2,128)} %param.10) | copy-start | bytes 3076
  7.2 38.5 %copy-start.2 = (bf16[128,1024]{1,0:T(8,128)(2,1)S(1)}, bf16[128,1024]{1,0:T(8,128)(2,1)}, u32[]{:S(2)}) copy-start(bf16[128,1024]{1,0:T(8,128)(2,1)} %param.13) | copy-start | bytes 786436
  7.2 68.2 %all-gather.3.cloned.1.call-start = ((), (), s32[]{:S(2)}) async-start(), calls=%async_computation.6 | async-start | bytes 2621440 | tf_op jit(solution)/shard_map/all_gather | solution.py:61
  45.3 66.0 %all-gather.5.cloned.1.call-start = ((), (), s32[]{:S(2)}) async-start(), calls=%async_computation.8 | async-start | bytes 2621440 | tf_op jit(solution)/shard_map/all_gather | solution.py:61
  73.6 73.2 %reduce-scatter.3.cloned.1.call-start = ((), (), s32[]{:S(2)}) async-start(), calls=%async_computation.7 | async-start | bytes 2621440 | tf_op jit(solution)/shard_map/reduce_scatter | solution.py:65
  80.0 1.9 copy-start.8
  85.9 96.1 %reduce-scatter.5.cloned.1.call-start = ((), (), s32[]{:S(2)}) async-start(), calls=%async_computation.9 | async-start | bytes 2621440 | tf_op jit(solution)/shard_map/reduce_scatter | solution.py:65
  111.3 8.6 %copy-start.6 = (bf16[1,1024,1024]{2,1,0:T(8,128)(2,1)S(1)}, bf16[1,1024,1024]{2,1,0:T(8,128)(2,1)}, u32[]{:S(2)}) copy-start(bf16[1,1024,1024]{2,1,0:T(8,128)(2,1)} %param.11) | copy-start | bytes 6291460
  118.5 1.4 copy-start.10
  123.6 36.0 %copy-start.4 = (s32[128,2]{0,1:T(2,128)S(1)}, s32[128,2]{0,1:T(2,128)}, u32[]{:S(2)}) copy-start(s32[128,2]{0,1:T(2,128)} %param.9) | copy-start | bytes 3076
  148.8 35.2 %all-to-all-start.1 = ((bf16[64,4,1024]{2,1,0:T(4,128)(2,1)}), bf16[64,4,1024]{2,1,0:T(4,128)(2,1)S(1)}, u32[]{:S(2)}, u32[]{:S(2)}) async-start(bf16[64,4,1024]{2,1,0:T(4,128)(2,1)} %reshape.122), calls=%async_computation.2 | async-start | bytes 1048576 | tf_op jit(solution)/shard_map/all_to_all | solution.py:68
  184.1 28.3 %all-to-all-start.3 = ((bf16[64,4,1024]{2,1,0:T(4,128)(2,1)}), bf16[64,4,1024]{2,1,0:T(4,128)(2,1)S(1)}, u32[]{:S(2)}, u32[]{:S(2)}) async-start(bf16[64,4,1024]{2,1,0:T(4,128)(2,1)} %reshape.126), calls=%async_computation.5 | async-start | bytes 1048576 | tf_op jit(solution)/shard_map/all_to_all | solution.py:68
  194.7 6.1 %copy-start.7 = (bf16[1024,1024]{1,0:T(8,128)(2,1)S(1)}, bf16[1024,1024]{1,0:T(8,128)(2,1)}, u32[]{:S(2)}) copy-start(bf16[1024,1024]{1,0:T(8,128)(2,1)} %all-gather.5.cloned.1.call-done) | copy-start | bytes 6291460
  194.7 6.1 %copy-start.9 = (f32[1024,1024]{1,0:T(8,128)S(1)}, f32[1024,1024]{1,0:T(8,128)}, u32[]{:S(2)}) copy-start(f32[1024,1024]{1,0:T(8,128)} %copy-done.8) | copy-start | bytes 12582916
  204.9 8.0 %copy-start.1 = (bf16[128,1024]{1,0:T(8,128)(2,1)S(1)}, bf16[128,1024]{1,0:T(8,128)(2,1)}, u32[]{:S(2)}) copy-start(bf16[128,1024]{1,0:T(8,128)(2,1)} %param.7) | copy-start | bytes 786436
  204.9 8.0 %copy-start.3 = (f32[1024]{0:T(1024)S(1)}, f32[1024]{0:T(1024)}, u32[]{:S(2)}) copy-start(f32[1024]{0:T(1024)} %param.8) | copy-start | bytes 12292
Sparse Core Ops, SparseCore 0:
  45.5 29.9 all-gather.2
  77.8 33.4 all-gather.4
  114.4 32.3 reduce-scatter.2
  150.0 32.0 reduce-scatter.4
where the time goes:
time: 223 us; the launch traced here: 222 us
  waiting for transfers between devices  76.8 us (34%)
  blocking collectives  53.7 us (24%)
  matrix products  34 us (15%)
  starting transfers between devices  21.6 us (10%)
  local copies, waits for them, and re-layouts  15.1 us (7%)
  between operations  14 us (6%)
  other arithmetic  6.86 us (3%)
    all_to_all x2, blocking collectives, arrive(): lax.all_to_all(sent, 'exp', split_axis=0, concat_axis=0, tiled=True)  53.7 us
    reduce_scatter x2, waiting for transfers between devices, depart(): lax.psum_scatter(partial_value.astype(jnp.bfloat16), 'rep', scatter_dimen...  45.4 us
    all_gather x2, waiting for transfers between devices, arrive(): lax.all_gather(landed.reshape(-1, landed.shape[-1]), 'rep', axis=0, tiled...  26.9 us
    all_to_all x2, starting transfers between devices, depart(): lax.all_to_all(summed.reshape(experts, capacity, summed.shape[-1]), 'exp'...  21.2 us
    dot_general x1, matrix products, expert_backward(): jnp.einsum('rd,fd->rf', grad_rows, w_second, preferred_element_type=jnp.f...  7.16 us
    dot_general x1, matrix products, expert_backward(): jnp.einsum('rd,rf->df', in_rows, d_pre, preferred_element_type=jnp.float32)  6.08 us
    dot_general x1, matrix products, expert_forward(): preact = jnp.dot(in_rows, w_first, preferred_element_type=jnp.float32)  4.55 us
  transfers between devices with their start and end apart: 6, of which 5 were waited for; matrix products, arithmetic and copies ran while one was open for 19% of the time, Pallas kernels for 0%

commit v1 on v0

v1 whole, which is shorter than its diff:
```python
import functools
import math

import jax
import jax.numpy as jnp
from jax import lax
from jax.experimental import pallas as pl
from jax.experimental.pallas import tpu as pltpu
from jax.sharding import PartitionSpec as P

MESH = pl.DeviceIdType.MESH
F32 = jnp.float32
BF16 = jnp.bfloat16
EPSILON = 1e-05
CAP = 4
UNIT = 2 * CAP
REPS = 4
PLANE = 8
ORDERS = {8: (0, 2, 6, 3, 5, 4, 1, 7), 4: (0, 2, 3, 1), 2: (0, 1)}
ROOT = math.sqrt(2.0 / math.pi)
CUBIC = 0.044715


def dot(left, right, contract=((1,), (0,))):
    return lax.dot_general(left, right, (contract, ((), ())), preferred_element_type=F32)


def kernel(
    order, plane, tile,
    tokens_ref, gain_ref, ids_ref, gates_ref, cot_ref, w_in_ref, w_out_ref,
    mixed_ref, grad_tokens_ref, grad_in_ref, grad_out_ref,
    w_first, w_second, sent, landed, gathered, x_rows, d_rows, hidden, d_pre,
    partial, relay, arrived, back, returned, disp, take, rows_in, xhat, scale, total, g_first, g_second,
    load_sem, disp_send, disp_recv, ag_send, ag_recv, fw_send, fw_recv,
    r1_send, r1_recv, r2_send, r2_recv, ret_send, ret_recv, store_sem,
):
    steps = len(order)
    toks, width = tokens_ref.shape
    group = plane * CAP
    both = 2 * group
    chunk = 2 * REPS * group
    chunks = steps // 2
    places = steps * plane * UNIT
    me_y = lax.axis_index("rep")
    me_e = lax.axis_index("exp")
    me_z = lax.div(me_e, plane)
    me_p = lax.rem(me_e, plane)
    experts = steps * plane
    up = {"rep": lax.rem(me_y + 1, REPS)}
    down = {"rep": lax.rem(me_y + REPS - 1, REPS)}
    sides = (up, down)

    load_first = pltpu.make_async_copy(w_in_ref, w_first, load_sem.at[0])
    load_second = pltpu.make_async_copy(w_out_ref, w_second, load_sem.at[1])
    load_first.start()
    load_second.start()

    barrier = pltpu.get_barrier_semaphore()

    @pl.loop(1, experts)
    def _(s):
        pl.semaphore_signal(barrier, inc=1, device_id={"exp": lax.rem(me_e + s, experts)}, device_id_type=MESH)

    for side in sides:
        pl.semaphore_signal(barrier, inc=1, device_id=side, device_id_type=MESH)

    values = tokens_ref[...].astype(F32)
    center = values - jnp.mean(values, axis=-1, keepdims=True)
    inv = lax.rsqrt(jnp.mean(center * center, axis=-1, keepdims=True) + EPSILON)
    unit = center * inv
    xhat[...] = unit
    scale[...] = inv
    rows_in[0:toks, :] = (unit * gain_ref[...]).astype(BF16)
    cot = cot_ref[...].astype(F32)
    for k in range(2):
        rows_in[(k + 1) * toks:(k + 2) * toks, :] = (cot * gates_ref[:, k:k + 1]).astype(BF16)

    def place_of(k):
        ids = ids_ref[:, k:k + 1]
        z = lax.rem(lax.div(ids, plane) - me_z + steps, steps)
        position = jnp.zeros_like(z)
        for i, away in enumerate(order):
            position = jnp.where(z == away, i, position)
        return position * plane + lax.rem(ids, plane)

    rel = [place_of(k) for k in range(2)]
    labels = lax.broadcasted_iota(jnp.int32, (toks, experts), 1)
    one = [(labels == r).astype(F32) for r in rel]
    earlier = (
        lax.broadcasted_iota(jnp.int32, (toks, toks), 1) < lax.broadcasted_iota(jnp.int32, (toks, toks), 0)
    ).astype(F32).astype(BF16)
    before = dot(earlier, (one[0] + one[1]).astype(BF16))
    q = lax.broadcasted_iota(jnp.int32, (toks, places), 1)
    pick_x, pick_d = [], []
    for k in range(2):
        rank = jnp.sum(before * one[k], axis=1, keepdims=True).astype(jnp.int32)
        target = jnp.where(rank < CAP, rel[k] * UNIT + rank, -UNIT)
        pick_x.append((q == target).astype(F32))
        pick_d.append((q == target + CAP).astype(F32))
    take[0:toks, :] = pick_x[0].astype(BF16)
    take[toks:2 * toks, :] = pick_x[1].astype(BF16)
    take[2 * toks:3 * toks, :] = (pick_d[0] + pick_d[1]).astype(BF16)
    disp[:, 0:toks] = (pick_x[0] + pick_x[1]).T.astype(BF16)
    disp[:, toks:2 * toks] = pick_d[0].T.astype(BF16)
    disp[:, 2 * toks:3 * toks] = pick_d[1].T.astype(BF16)

    def peer(away, p):
        return {"exp": lax.rem(me_z + away + steps, steps) * plane + p}

    rows_at = plane * UNIT

    def dispatch(i):
        piece = dot(disp[i * rows_at:(i + 1) * rows_at, :], rows_in[...])
        sent[i] = piece.reshape(plane, UNIT, width).astype(BF16)
        if i == 0:
            pl.semaphore_wait(barrier, experts - 1 + 2)
        away = order[i]
        if away == 0:
            pltpu.make_async_copy(sent.at[i, me_p], landed.at[i, me_p], disp_recv.at[i]).start()

        @pl.loop(1 if away == 0 else 0, plane)
        def _(s):
            p = lax.rem(me_p + s, plane)
            pltpu.make_async_remote_copy(
                sent.at[i, p], landed.at[i, me_p], disp_send.at[i], disp_recv.at[i],
                device_id=peer(away, p), device_id_type=MESH,
            ).start()

    r = lax.broadcasted_iota(jnp.int32, (both, both), 0)
    c = lax.broadcasted_iota(jnp.int32, (both, both), 1)

    def mixed_row(pure):
        kind = lax.div(pure, group)
        row = lax.rem(pure, group)
        return lax.div(row, CAP) * UNIT + kind * CAP + lax.rem(row, CAP)

    def split_perm():
        return (c == mixed_row(r)).astype(F32).astype(BF16)

    def merge_perm():
        return (r == mixed_row(c)).astype(F32).astype(BF16)

    def whole(ref, sem):
        pltpu.make_async_copy(ref, ref, sem).wait()

    def remote(src, dst, send, recv, where):
        return pltpu.make_async_remote_copy(src, dst, send, recv, device_id=where, device_id_type=MESH)

    def arrive(i):
        whole(landed.at[i], disp_recv.at[i])
        units = landed[i].astype(F32).reshape(both, width).astype(BF16)
        gathered[0, i] = dot(split_perm(), units).astype(BF16)
        for s, slot in ((0, 1), (1, 3)):
            remote(gathered.at[0, i], gathered.at[slot, i], ag_send.at[s], ag_recv.at[s, i], sides[s]).start()

    def forward(i):
        for s, slot in ((0, 1), (1, 3)):
            whole(gathered.at[slot, i], ag_recv.at[s, i])
            half = pl.ds(s * group, group)
            remote(
                gathered.at[slot, i, half], gathered.at[2, i, half], fw_send.at[s], fw_recv.at[s, i], sides[s]
            ).start()

    def complete(i):
        for s in range(2):
            whole(gathered.at[2, i, pl.ds(s * group, group)], fw_recv.at[s, i])

    def pack(n):
        for rel_y in range(REPS):
            for b in range(2):
                at = n * chunk + (rel_y * 2 + b) * group
                x_rows[at:at + group, :] = gathered[rel_y, 2 * n + b, 0:group, :]
                d_rows[at:at + group, :] = gathered[rel_y, 2 * n + b, group:both, :]

    ff = w_first.shape[1]

    def first_half(n, lo, hi):
        here = pl.ds(n * chunk, chunk)

        @pl.loop(lo, hi)
        def _(t):
            cols = pl.ds(pl.multiple_of(t * tile, tile), tile)
            v = dot(x_rows[here, :], w_first[:, cols])
            g = dot(d_rows[here, :], w_second[cols, :], ((1,), (1,)))
            square = v * v
            th = jnp.tanh(v * (ROOT + (ROOT * CUBIC) * square))
            half_up = 0.5 + 0.5 * th
            hidden[here, cols] = (v * half_up).astype(BF16)
            slope = half_up + (0.5 * v) * (1.0 - th * th) * (ROOT + (3.0 * ROOT * CUBIC) * square)
            d_pre[here, cols] = (g * slope).astype(BF16)

    def second_half(n, lo, hi):
        here = pl.ds(n * chunk, chunk)

        @pl.loop(lo, hi)
        def _(t):
            cols = pl.ds(pl.multiple_of(t * tile, tile), tile)
            y = dot(hidden[here, :], w_second[:, cols]).astype(BF16)
            dx = dot(d_pre[here, :], w_first[cols, :], ((1,), (1,))).astype(BF16)
            for rel_y in range(REPS):
                for b in range(2):
                    at = (rel_y * 2 + b) * group
                    partial[rel_y, 2 * n + b, 0:group, cols] = y[at:at + group]
                    partial[rel_y, 2 * n + b, group:both, cols] = dx[at:at + group]

    opposite = (3, 1)

    def reduce_first(i):
        for s in range(2):
            half = pl.ds(s * group, group)
            other = pl.ds((1 - s) * group, group)
            remote(partial.at[2, i, half], relay.at[s, i], r1_send.at[s], r1_recv.at[s, i], sides[s]).start()
            remote(
                partial.at[opposite[s], i, other], arrived.at[s, i, other], r2_send.at[s], r2_recv.at[s, i], sides[s]
            ).start()

    def reduce_second(i):
        for s in range(2):
            half = pl.ds(s * group, group)
            whole(relay.at[s, i], r1_recv.at[s, i])
            summed = partial[opposite[s], i, half, :].astype(F32) + relay[s, i].astype(F32)
            partial[opposite[s], i, half, :] = summed.astype(BF16)
            remote(
                partial.at[opposite[s], i, half], arrived.at[s, i, half], r2_send.at[s], r2_recv.at[s, i], sides[s]
            ).start()

    def give_back(i):
        for s in range(2):
            whole(arrived.at[s, i], r2_recv.at[s, i])
        summed = partial[0, i].astype(F32) + arrived[0, i].astype(F32) + arrived[1, i].astype(F32)
        back[i] = dot(merge_perm(), summed.astype(BF16)).reshape(plane, UNIT, width).astype(BF16)
        away = order[i]
        if away == 0:
            pltpu.make_async_copy(back.at[i, me_p], returned.at[i, me_p], ret_recv.at[i]).start()

        @pl.loop(1 if away == 0 else 0, plane)
        def _(s):
            p = lax.rem(me_p + s, plane)
            remote(
                back.at[i, p], returned.at[i, me_p], ret_send.at[i], ret_recv.at[i], peer(-away, p)
            ).start()

    def combine(n):
        for b in range(2):
            whole(returned.at[2 * n + b], ret_recv.at[2 * n + b])
        span = 2 * rows_at
        units = returned[2 * n:2 * n + 2].astype(F32).reshape(span, width).astype(BF16)
        got = dot(take[:, n * span:(n + 1) * span], units)
        if n == 0:
            total[...] = got
        else:
            total[...] += got

    stores = []

    def weights_out():
        @pl.loop(0, ff // tile)
        def _(t):
            cols = pl.ds(pl.multiple_of(t * tile, tile), tile)
            g_second[cols, :] = dot(hidden[:, cols], d_rows[...], ((0,), (0,))).astype(BF16)

        stores.append(pltpu.make_async_copy(g_second, grad_out_ref, store_sem.at[1]))
        stores[-1].start()

        @pl.loop(0, width // tile)
        def _(t):
            cols = pl.ds(pl.multiple_of(t * tile, tile), tile)
            g_first[cols, :] = dot(x_rows[:, cols], d_pre[...], ((0,), (0,))).astype(BF16)

        stores.append(pltpu.make_async_copy(g_first, grad_in_ref, store_sem.at[0]))
        stores[-1].start()

    tiles = ff // tile
    for i in range(steps):
        dispatch(i)
    load_first.wait()
    load_second.wait()
    arrive(0)
    arrive(1)
    forward(0)
    forward(1)
    for n in range(chunks):
        last = n == chunks - 1
        if not last:
            arrive(2 * n + 2)
        complete(2 * n)
        complete(2 * n + 1)
        pack(n)
        first_half(n, 0, tiles // 2)
        if not last:
            arrive(2 * n + 3)
        if n:
            reduce_second(2 * n - 2)
            reduce_second(2 * n - 1)
        first_half(n, tiles // 2, tiles)
        if not last:
            forward(2 * n + 2)
        second_half(n, 0, tiles // 2)
        if n:
            give_back(2 * n - 2)
        if not last:
            forward(2 * n + 3)
        second_half(n, tiles // 2, tiles)
        reduce_first(2 * n)
        reduce_first(2 * n + 1)
        if n:
            give_back(2 * n - 1)
    n = chunks - 1
    reduce_second(2 * n)
    reduce_second(2 * n + 1)
    weights_out()
    for i in (2 * n, 2 * n + 1):
        give_back(i)
    for n in range(chunks):
        combine(n)

    picked = total[0:toks, :] * gates_ref[:, 0:1] + total[toks:2 * toks, :] * gates_ref[:, 1:2]
    mixed_ref[...] = (tokens_ref[...].astype(F32) + picked).astype(BF16)
    g = total[2 * toks:3 * toks, :] * gain_ref[...]
    unit = xhat[...]
    inner = g - jnp.mean(g, axis=-1, keepdims=True) - unit * jnp.mean(g * unit, axis=-1, keepdims=True)
    grad_tokens_ref[...] = (cot_ref[...].astype(F32) + scale[...] * inner).astype(BF16)

    for i in range(steps):
        for buf, sem in ((sent, disp_send), (back, ret_send)):
            whole(buf.at[i, 0:plane - 1] if order[i] == 0 else buf.at[i], sem.at[i])
    for s in range(2):
        whole(gathered.at[0], ag_send.at[s])
        whole(gathered.at[0, :, pl.ds(0, group)], fw_send.at[s])
        whole(partial.at[0, :, pl.ds(0, group)], r1_send.at[s])
        whole(partial.at[0], r2_send.at[s])
    for store in stores:
        store.wait()


def local(plane, tokens, gain, expert_ids, gates, w_in, w_out, cotangent):
    experts = lax.axis_size("exp")
    steps = experts // plane
    order = ORDERS[steps]
    toks, width = tokens.shape
    ff = w_in.shape[2]
    group = plane * CAP
    rows = experts * CAP * REPS
    places = experts * UNIT
    dma = pltpu.SemaphoreType.DMA
    vmem = pl.BlockSpec(memory_space=pltpu.VMEM)
    hbm = pl.BlockSpec(memory_space=pl.ANY)
    unit = (steps, plane, UNIT, width)
    mixed, grad_tokens, grad_in, grad_out = pl.pallas_call(
        functools.partial(kernel, order, plane, min(256, ff // 2)),
        out_shape=(
            jax.ShapeDtypeStruct((toks, width), BF16),
            jax.ShapeDtypeStruct((toks, width), BF16),
            jax.ShapeDtypeStruct((width, ff), BF16),
            jax.ShapeDtypeStruct((ff, width), BF16),
        ),
        in_specs=[vmem] * 5 + [hbm] * 2,
        out_specs=(vmem, vmem, hbm, hbm),
        scratch_shapes=[
            pltpu.VMEM((width, ff), BF16),
            pltpu.VMEM((ff, width), BF16),
            pltpu.VMEM(unit, BF16),
            pltpu.VMEM(unit, BF16),
            pltpu.VMEM((REPS, steps, 2 * group, width), BF16),
            pltpu.VMEM((rows, width), BF16),
            pltpu.VMEM((rows, width), BF16),
            pltpu.VMEM((rows, ff), BF16),
            pltpu.VMEM((rows, ff), BF16),
            pltpu.VMEM((REPS, steps, 2 * group, width), BF16),
            pltpu.VMEM((2, steps, group, width), BF16),
            pltpu.VMEM((2, steps, 2 * group, width), BF16),
            pltpu.VMEM(unit, BF16),
            pltpu.VMEM(unit, BF16),
            pltpu.VMEM((places, 3 * toks), BF16),
            pltpu.VMEM((3 * toks, places), BF16),
            pltpu.VMEM((3 * toks, width), BF16),
            pltpu.VMEM((toks, width), F32),
            pltpu.VMEM((toks, 1), F32),
            pltpu.VMEM((3 * toks, width), F32),
            pltpu.VMEM((width, ff), BF16),
            pltpu.VMEM((ff, width), BF16),
            dma((2,)),
            dma((steps,)),
            dma((steps,)),
            dma((2,)),
            dma((2, steps)),
            dma((2,)),
            dma((2, steps)),
            dma((2,)),
            dma((2, steps)),
            dma((2,)),
            dma((2, steps)),
            dma((steps,)),
            dma((steps,)),
            dma((2,)),
        ],
        compiler_params=pltpu.CompilerParams(
            collective_id=0, has_side_effects=True, vmem_limit_bytes=56 * 1024 * 1024
        ),
    )(tokens, gain.reshape(1, width), expert_ids, gates, cotangent, w_in[0], w_out[0])
    return (mixed, grad_tokens, grad_in[None], grad_out[None])


def solution(mesh, plane=PLANE):
    return jax.shard_map(
        functools.partial(local, plane),
        mesh=mesh,
        in_specs=(
            P(("rep", "exp"), None),
            P(),
            P(("rep", "exp"), None),
            P(("rep", "exp"), None),
            P("exp", None, "rep"),
            P("exp", "rep", None),
            P(("rep", "exp"), None),
        ),
        out_specs=(
            P(("rep", "exp"), None),
            P(("rep", "exp"), None),
            P("exp", None, "rep"),
            P("exp", "rep", None),
        ),
        check_vma=False,
    )
```

time: 223 us -> 116 us (0.52)
  Pallas kernels: 0 us -> 105 us
  waiting for transfers between devices: 76.8 us -> 0 us
  blocking collectives: 53.7 us -> 0 us
  matrix products: 34 us -> 0 us
  starting transfers between devices: 21.6 us -> 0 us
  between operations: 14 us -> 0.64 us
  other arithmetic: 6.86 us -> 0 us
  local copies, waits for them, and re-layouts: 15.1 us -> 10.7 us
    pallas_call x0 -> x1, Pallas kernels: none -> 105 us  [local(): pl.pallas_call(functools.partial(kernel, order, plane, min(256, ff // 2))...]
    all_to_all x2 -> x0, blocking collectives: 53.7 us -> none  [arrive(): lax.all_to_all(sent, 'exp', split_axis=0, concat_axis=0, tiled=True)]
    reduce_scatter x2 -> x0, waiting for transfers between devices: 45.4 us -> none  [depart(): lax.psum_scatter(partial_value.astype(jnp.bfloat16), 'rep', scatter_dimen...]
    dot_general x10 -> x0, matrix products: 34 us -> none  [the longest x1 7.16 us: expert_backward(): jnp.einsum('rd,fd->rf', grad_rows, w_second, preferred_element_type=jnp.f...]
    all_gather x2 -> x0, waiting for transfers between devices: 26.9 us -> none  [arrive(): lax.all_gather(landed.reshape(-1, landed.shape[-1]), 'rep', axis=0, tiled...]
    all_to_all x2 -> x0, starting transfers between devices: 21.2 us -> none  [depart(): lax.all_to_all(summed.reshape(experts, capacity, summed.shape[-1]), 'exp'...]
    reshape x9 -> x0, local copies, waits for them, and re-layouts: 7.57 us -> none  [the longest x2 4.09 us: depart(): summed.reshape(experts, capacity, summed.shape[-1])]
    unnamed x24 -> x8, local copies, waits for them, and re-layouts: 4.4 us -> 10.7 us
  transfers between devices with their start and end apart: 6 -> 0, of which waited for: 5 -> 0; matrix products, arithmetic and copies ran while one was open for 19% -> 0% of each run, Pallas kernels for 0% -> 0%
where the time goes in v1:
time: 116 us
  Pallas kernels  105 us (91%)
  local copies, waits for them, and re-layouts  10.7 us (9%)
    pallas_call x1, Pallas kernels, local(): pl.pallas_call(functools.partial(kernel, order, plane, min(256, ff // 2))...  105 us
    unnamed x8, local copies, waits for them, and re-layouts  10.7 us

profile of v1, /device:TPU:1, one launch (start us, length us, event | category | flops | bytes accessed | tf_op | source)
XLA Modules:
  0.0 116.2 jit_solution(123388310299296791)
XLA Ops:
  0.6 1.4 %copy.11.ids_ref = s32[128,2]{1,0:T(8,128)} copy(s32[128,2]{0,1:T(2,128)} %param.9) | data formatting | bytes 2048 | tf_op args[2]
  2.0 1.4 %copy.12.gates_ref = f32[128,2]{1,0:T(8,128)} copy(f32[128,2]{0,1:T(2,128)} %param.10) | data formatting | bytes 2048 | tf_op args[3]
  3.5 104.9 %shard_map.102 = (bf16[128,1024]{1,0:T(8,128)(2,1)}, bf16[128,1024]{1,0:T(8,128)(2,1)}, bf16[1024,1024]{1,0:T(8,128)(2,1)}, bf16[1024,1024]{1,0:T(8,128)(2,1)}) custom-call(bf16[128,1024]{1,0:T(8,128)(2,1)} %tokens_ref.1, f32[1,1024]{1,0:T(1,128)} %bitcast.9, s32[128,2]{1,0:T(8,128)} %copy.11.ids_ref, f32[128,2]{1,0:T(8,128)} %copy.12.gates_ref, ...), custom_call_target="tpu_custom_call" | custom-call | tf_op jit(solution)/shard_map/pallas_call | solution.py:349
  108.3 1.7 %copy.17 = bf16[128,1024]{1,0:T(8,128)(2,1)} copy(bf16[128,1024]{1,0:T(8,128)(2,1)} %get-tuple-element.16) | data formatting | bytes 524288
  110.0 1.7 %copy.18 = bf16[128,1024]{1,0:T(8,128)(2,1)} copy(bf16[128,1024]{1,0:T(8,128)(2,1)} %get-tuple-element.17) | data formatting | bytes 524288
  111.7 0.0 copy-start
  111.7 3.2 %copy.19 = bf16[1,1024,1024]{2,1,0:T(8,128)(2,1)} copy(bf16[1,1024,1024]{2,1,0:T(8,128)(2,1)} %bitcast.8) | data formatting | bytes 4194304
  114.9 0.0 copy-done
  114.9 1.3 %copy.20 = bf16[1,1024,1024]{2,1,0:T(8,128)(2,1)} copy(bf16[1,1024,1024]{2,1,0:T(8,128)(2,1)S(1)} %bitcast.7) | data formatting | bytes 4194304
Async XLA Ops:
  111.7 3.2 %copy-start = (bf16[1024,1024]{1,0:T(8,128)(2,1)S(1)}, bf16[1024,1024]{1,0:T(8,128)(2,1)}, u32[]{:S(2)}) copy-start(bf16[1024,1024]{1,0:T(8,128)(2,1)} %get-tuple-element.11) | copy-start | bytes 6291460

commit v2 on v1

--- a/solution.py
+++ b/solution.py
@@ -16,7 +16,7 @@
 UNIT = 2 * CAP
 REPS = 4
 PLANE = 8
-ORDERS = {8: (0, 2, 6, 3, 5, 4, 1, 7), 4: (0, 2, 3, 1), 2: (0, 1)}
+ORDERS = {8: (0, 1, 2, 6, 3, 5, 4, 7), 4: (0, 1, 2, 3), 2: (0, 1)}
 ROOT = math.sqrt(2.0 / math.pi)
 CUBIC = 0.044715
 
@@ -27,12 +27,12 @@
 
 def kernel(
     order, plane, tile,
-    tokens_ref, gain_ref, ids_ref, gates_ref, cot_ref, w_in_ref, w_out_ref,
-    mixed_ref, grad_tokens_ref, grad_in_ref, grad_out_ref,
+    tokens_hbm, gain_ref, ids_ref, gates_ref, cot_hbm, w_in_ref, w_out_ref,
+    total, tokens_ref, cot_ref, xhat, scale, columns, g_first, g_second,
     w_first, w_second, sent, landed, gathered, x_rows, d_rows, hidden, d_pre,
-    partial, relay, arrived, back, returned, disp, take, rows_in, xhat, scale, total, g_first, g_second,
+    partial, relay, arrived, back, returned, disp, take, rows_in,
     load_sem, disp_send, disp_recv, ag_send, ag_recv, fw_send, fw_recv,
-    r1_send, r1_recv, r2_send, r2_recv, ret_send, ret_recv, store_sem,
+    r1_send, r1_recv, r2_send, r2_recv, ret_send, ret_recv,
 ):
     steps = len(order)
     toks, width = tokens_ref.shape
@@ -50,20 +50,55 @@
     down = {"rep": lax.rem(me_y + REPS - 1, REPS)}
     sides = (up, down)
 
-    load_first = pltpu.make_async_copy(w_in_ref, w_first, load_sem.at[0])
-    load_second = pltpu.make_async_copy(w_out_ref, w_second, load_sem.at[1])
-    load_first.start()
-    load_second.start()
+    loads = [
+        pltpu.make_async_copy(src, dst, load_sem.at[j])
+        for j, (src, dst) in enumerate(
+            ((tokens_hbm, tokens_ref), (cot_hbm, cot_ref), (w_in_ref, w_first), (w_out_ref, w_second))
+        )
+    ]
+    loads[0].start()
+    loads[1].start()
 
     barrier = pltpu.get_barrier_semaphore()
+    for side in sides:
+        pl.semaphore_signal(barrier, inc=1, device_id=side, device_id_type=MESH)
 
     @pl.loop(1, experts)
     def _(s):
         pl.semaphore_signal(barrier, inc=1, device_id={"exp": lax.rem(me_e + s, experts)}, device_id_type=MESH)
 
-    for side in sides:
-        pl.semaphore_signal(barrier, inc=1, device_id=side, device_id_type=MESH)
-
+    loads[2].start()
+    loads[3].start()
+
+    def place_of(k):
+        ids = ids_ref[k:k + 1, :]
+        z = lax.rem(lax.div(ids, plane) - me_z + steps, steps)
+        position = jnp.zeros_like(z)
+        for i, away in enumerate(order):
+            position = jnp.where(z == away, i, position)
+        return position * plane + lax.rem(ids, plane)
+
+    rel = [place_of(k) for k in range(2)]
+    labels = lax.broadcasted_iota(jnp.int32, (experts, toks), 0)
+    one = [(labels == r).astype(F32) for r in rel]
+    earlier = (
+        lax.broadcasted_iota(jnp.int32, (toks, toks), 0) < lax.broadcasted_iota(jnp.int32, (toks, toks), 1)
+    ).astype(F32).astype(BF16)
+    before = dot((one[0] + one[1]).astype(BF16), earlier)
+    targets = []
+    for k in range(2):
+        rank = jnp.sum(before * one[k], axis=0, keepdims=True).astype(jnp.int32)
+        targets.append(jnp.where(rank < CAP, rel[k] * UNIT + rank, -UNIT))
+    table = jnp.concatenate(
+        [t.astype(F32) for t in targets] + [gates_ref[...], jnp.zeros((4, toks), F32)], axis=0
+    ).T
+    columns[...] = table
+    down_q = lax.broadcasted_iota(jnp.int32, (places, toks), 0)
+    disp[:, 0:toks] = ((down_q == targets[0]) | (down_q == targets[1])).astype(F32).astype(BF16)
+    for k in range(2):
+        disp[:, (k + 1) * toks:(k + 2) * toks] = (down_q == targets[k] + CAP).astype(F32).astype(BF16)
+
+    loads[0].wait()
     values = tokens_ref[...].astype(F32)
     center = values - jnp.mean(values, axis=-1, keepdims=True)
     inv = lax.rsqrt(jnp.mean(center * center, axis=-1, keepdims=True) + EPSILON)
@@ -71,38 +106,19 @@
     xhat[...] = unit
     scale[...] = inv
     rows_in[0:toks, :] = (unit * gain_ref[...]).astype(BF16)
+    loads[1].wait()
     cot = cot_ref[...].astype(F32)
     for k in range(2):
-        rows_in[(k + 1) * toks:(k + 2) * toks, :] = (cot * gates_ref[:, k:k + 1]).astype(BF16)
-
-    def place_of(k):
-        ids = ids_ref[:, k:k + 1]
-        z = lax.rem(lax.div(ids, plane) - me_z + steps, steps)
-        position = jnp.zeros_like(z)
-        for i, away in enumerate(order):
-            position = jnp.where(z == away, i, position)
-        return position * plane + lax.rem(ids, plane)
-
-    rel = [place_of(k) for k in range(2)]
-    labels = lax.broadcasted_iota(jnp.int32, (toks, experts), 1)
-    one = [(labels == r).astype(F32) for r in rel]
-    earlier = (
-        lax.broadcasted_iota(jnp.int32, (toks, toks), 1) < lax.broadcasted_iota(jnp.int32, (toks, toks), 0)
-    ).astype(F32).astype(BF16)
-    before = dot(earlier, (one[0] + one[1]).astype(BF16))
-    q = lax.broadcasted_iota(jnp.int32, (toks, places), 1)
-    pick_x, pick_d = [], []
-    for k in range(2):
-        rank = jnp.sum(before * one[k], axis=1, keepdims=True).astype(jnp.int32)
-        target = jnp.where(rank < CAP, rel[k] * UNIT + rank, -UNIT)
-        pick_x.append((q == target).astype(F32))
-        pick_d.append((q == target + CAP).astype(F32))
-    take[0:toks, :] = pick_x[0].astype(BF16)
-    take[toks:2 * toks, :] = pick_x[1].astype(BF16)
-    take[2 * toks:3 * toks, :] = (pick_d[0] + pick_d[1]).astype(BF16)
-    disp[:, 0:toks] = (pick_x[0] + pick_x[1]).T.astype(BF16)
-    disp[:, toks:2 * toks] = pick_d[0].T.astype(BF16)
-    disp[:, 2 * toks:3 * toks] = pick_d[1].T.astype(BF16)
+        rows_in[(k + 1) * toks:(k + 2) * toks, :] = (cot * table[:, 2 + k:3 + k]).astype(BF16)
+
+    def write_take():
+        across_q = lax.broadcasted_iota(jnp.int32, (toks, places), 1)
+        target = [columns[:, k:k + 1].astype(jnp.int32) for k in range(2)]
+        for k in range(2):
+            take[k * toks:(k + 1) * toks, :] = (across_q == target[k]).astype(F32).astype(BF16)
+        take[2 * toks:3 * toks, :] = (
+            (across_q == target[0] + CAP) | (across_q == target[1] + CAP)
+        ).astype(F32).astype(BF16)
 
     def peer(away, p):
         return {"exp": lax.rem(me_z + away + steps, steps) * plane + p}
@@ -205,14 +221,17 @@
 
     opposite = (3, 1)
 
-    def reduce_first(i):
-        for s in range(2):
-            half = pl.ds(s * group, group)
-            other = pl.ds((1 - s) * group, group)
-            remote(partial.at[2, i, half], relay.at[s, i], r1_send.at[s], r1_recv.at[s, i], sides[s]).start()
-            remote(
-                partial.at[opposite[s], i, other], arrived.at[s, i, other], r2_send.at[s], r2_recv.at[s, i], sides[s]
-            ).start()
+    def reduce_first(group_ids):
+        for i in group_ids:
+            for s in range(2):
+                half = pl.ds(s * group, group)
+                remote(partial.at[2, i, half], relay.at[s, i], r1_send.at[s], r1_recv.at[s, i], sides[s]).start()
+        for i in group_ids:
+            for s in range(2):
+                half = pl.ds((1 - s) * group, group)
+                remote(
+                    partial.at[opposite[s], i, half], arrived.at[s, i, half], r2_send.at[s], r2_recv.at[s, i], sides[s]
+                ).start()
 
     def reduce_second(i):
         for s in range(2):
@@ -251,75 +270,80 @@
         else:
             total[...] += got
 
-    stores = []
-
-    def weights_out():
-        @pl.loop(0, ff // tile)
+    def out_grad(lo, hi):
+        @pl.loop(lo, hi)
         def _(t):
             cols = pl.ds(pl.multiple_of(t * tile, tile), tile)
             g_second[cols, :] = dot(hidden[:, cols], d_rows[...], ((0,), (0,))).astype(BF16)
 
-        stores.append(pltpu.make_async_copy(g_second, grad_out_ref, store_sem.at[1]))
-        stores[-1].start()
-
-        @pl.loop(0, width // tile)
+    def in_grad(lo, hi):
+        @pl.loop(lo, hi)
         def _(t):
             cols = pl.ds(pl.multiple_of(t * tile, tile), tile)
             g_first[cols, :] = dot(x_rows[:, cols], d_pre[...], ((0,), (0,))).astype(BF16)
 
-        stores.append(pltpu.make_async_copy(g_first, grad_in_ref, store_sem.at[0]))
-        stores[-1].start()
-
     tiles = ff // tile
-    for i in range(steps):
+    cut = tiles // 2
+    ready = iter(range(steps))
+    passed = iter(range(steps))
+
+    def arrive_next():
+        i = next(ready, None)
+        if i is not None:
+            arrive(i)
+
+    def forward_next():
+        i = next(passed, None)
+        if i is not None:
+            forward(i)
+
+    early = min(4, steps)
+    dispatch(0)
+    dispatch(1)
+    arrive_next()
+    for i in range(2, early):
         dispatch(i)
-    load_first.wait()
-    load_second.wait()
-    arrive(0)
-    arrive(1)
-    forward(0)
-    forward(1)
+    arrive_next()
+    for i in range(early, steps):
+        dispatch(i)
+    forward_next()
+    arrive_next()
+    write_take()
+    forward_next()
+    arrive_next()
+    loads[2].wait()
+    loads[3].wait()
     for n in range(chunks):
-        last = n == chunks - 1
-        if not last:
-            arrive(2 * n + 2)
         complete(2 * n)
         complete(2 * n + 1)
         pack(n)
-        first_half(n, 0, tiles // 2)
-        if not last:
-            arrive(2 * n + 3)
+        first_half(n, 0, cut)
+        forward_next()
         if n:
             reduce_second(2 * n - 2)
+        first_half(n, cut, tiles)
+        arrive_next()
+        forward_next()
+        if n:
             reduce_second(2 * n - 1)
-        first_half(n, tiles // 2, tiles)
-        if not last:
-            forward(2 * n + 2)
-        second_half(n, 0, tiles // 2)
+        second_half(n, 0, cut)
+        arrive_next()
+        second_half(n, cut, tiles)
+        reduce_first((2 * n, 2 * n + 1))
         if n:
             give_back(2 * n - 2)
-        if not last:
-            forward(2 * n + 3)
-        second_half(n, tiles // 2, tiles)
-        reduce_first(2 * n)
-        reduce_first(2 * n + 1)
-        if n:
             give_back(2 * n - 1)
     n = chunks - 1
+    out_grad(0, cut)
     reduce_second(2 * n)
+    out_grad(cut, tiles)
     reduce_second(2 * n + 1)
-    weights_out()
-    for i in (2 * n, 2 * n + 1):
-        give_back(i)
+    in_grad(0, cut)
+    give_back(2 * n)
+    in_grad(cut, tiles)
+    give_back(2 * n + 1)
     for n in range(chunks):
         combine(n)
-
-    picked = total[0:toks, :] * gates_ref[:, 0:1] + total[toks:2 * toks, :] * gates_ref[:, 1:2]
-    mixed_ref[...] = (tokens_ref[...].astype(F32) + picked).astype(BF16)
-    g = total[2 * toks:3 * toks, :] * gain_ref[...]
-    unit = xhat[...]
-    inner = g - jnp.mean(g, axis=-1, keepdims=True) - unit * jnp.mean(g * unit, axis=-1, keepdims=True)
-    grad_tokens_ref[...] = (cot_ref[...].astype(F32) + scale[...] * inner).astype(BF16)
 
     for i in range(steps):
         for buf, sem in ((sent, disp_send), (back, ret_send)):
@@ -329,6 +353,29 @@
         whole(gathered.at[0, :, pl.ds(0, group)], fw_send.at[s])
         whole(partial.at[0, :, pl.ds(0, group)], r1_send.at[s])
         whole(partial.at[0], r2_send.at[s])
+
+
+def finish(
+    total, tokens_ref, cot_ref, xhat, scale, columns, g_first, g_second, gain_ref,
+    mixed_ref, grad_tokens_ref, grad_in_ref, grad_out_ref, mixed, grad_tokens, store_sem,
+):
+    toks = tokens_ref.shape[0]
+    stores = [
+        pltpu.make_async_copy(src, dst, store_sem.at[j])
+        for j, (src, dst) in enumerate((
+            (g_first, grad_in_ref), (g_second, grad_out_ref), (mixed, mixed_ref), (grad_tokens, grad_tokens_ref),
+        ))
+    ]
+    stores[0].start()
+    stores[1].start()
+    picked = total[0:toks, :] * columns[:, 2:3] + total[toks:2 * toks, :] * columns[:, 3:4]
+    mixed[...] = (tokens_ref[...].astype(F32) + picked).astype(BF16)
+    stores[2].start()
+    g = total[2 * toks:3 * toks, :] * gain_ref[...]
+    unit = xhat[...]
+    inner = g - jnp.mean(g, axis=-1, keepdims=True) - unit * jnp.mean(g * unit, axis=-1, keepdims=True)
+    grad_tokens[...] = (cot_ref[...].astype(F32) + scale[...] * inner).astype(BF16)
+    stores[3].start()
     for store in stores:
         store.wait()
 
@@ -346,16 +393,20 @@
     vmem = pl.BlockSpec(memory_space=pltpu.VMEM)
     hbm = pl.BlockSpec(memory_space=pl.ANY)
     unit = (steps, plane, UNIT, width)
-    mixed, grad_tokens, grad_in, grad_out = pl.pallas_call(
+    held = pl.pallas_call(
         functools.partial(kernel, order, plane, min(256, ff // 2)),
         out_shape=(
-            jax.ShapeDtypeStruct((toks, width), BF16),
-            jax.ShapeDtypeStruct((toks, width), BF16),
-            jax.ShapeDtypeStruct((width, ff), BF16),
-            jax.ShapeDtypeStruct((ff, width), BF16),
+            pltpu.VMEM((3 * toks, width), F32),
+            pltpu.VMEM((toks, width), BF16),
+            pltpu.VMEM((toks, width), BF16),
+            pltpu.VMEM((toks, width), F32),
+            pltpu.VMEM((toks, 1), F32),
+            pltpu.VMEM((toks, 8), F32),
+            pltpu.VMEM((width, ff), BF16),
+            pltpu.VMEM((ff, width), BF16),
         ),
-        in_specs=[vmem] * 5 + [hbm] * 2,
-        out_specs=(vmem, vmem, hbm, hbm),
+        in_specs=[hbm, vmem, vmem, vmem, hbm, hbm, hbm],
+        out_specs=(vmem,) * 8,
         scratch_shapes=[
             pltpu.VMEM((width, ff), BF16),
             pltpu.VMEM((ff, width), BF16),
@@ -374,12 +425,7 @@
             pltpu.VMEM((places, 3 * toks), BF16),
             pltpu.VMEM((3 * toks, places), BF16),
             pltpu.VMEM((3 * toks, width), BF16),
-            pltpu.VMEM((toks, width), F32),
-            pltpu.VMEM((toks, 1), F32),
-            pltpu.VMEM((3 * toks, width), F32),
-            pltpu.VMEM((width, ff), BF16),
-            pltpu.VMEM((ff, width), BF16),
-            dma((2,)),
+            dma((4,)),
             dma((steps,)),
             dma((steps,)),
             dma((2,)),
@@ -392,12 +438,28 @@
             dma((2, steps)),
             dma((steps,)),
             dma((steps,)),
-            dma((2,)),
         ],
         compiler_params=pltpu.CompilerParams(
-            collective_id=0, has_side_effects=True, vmem_limit_bytes=56 * 1024 * 1024
+            collective_id=0, has_side_effects=True, vmem_limit_bytes=53 * 1024 * 1024
         ),
-    )(tokens, gain.reshape(1, width), expert_ids, gates, cotangent, w_in[0], w_out[0])
+    )(tokens, gain.reshape(1, width), expert_ids.T, gates.T, cotangent, w_in[0], w_out[0])
+    mixed, grad_tokens, grad_in, grad_out = pl.pallas_call(
+        finish,
+        out_shape=(
+            jax.ShapeDtypeStruct((toks, width), BF16),
+            jax.ShapeDtypeStruct((toks, width), BF16),
+            jax.ShapeDtypeStruct((width, ff), BF16),
+            jax.ShapeDtypeStruct((ff, width), BF16),
+        ),
+        in_specs=[vmem] * 9,
+        out_specs=(hbm,) * 4,
+        scratch_shapes=[
+            pltpu.VMEM((toks, width), BF16),
+            pltpu.VMEM((toks, width), BF16),
+            dma((4,)),
+        ],
+        compiler_params=pltpu.CompilerParams(vmem_limit_bytes=16 * 1024 * 1024),
+    )(*[pltpu.with_memory_space_constraint(h, pltpu.VMEM) for h in held], gain.reshape(1, width))
     return (mixed, grad_tokens, grad_in[None], grad_out[None])
 
 

time: 116 us -> 108 us (0.931)
  local copies, waits for them, and re-layouts: 10.7 us -> 0.01 us
  Pallas kernels: 105 us -> 107 us
    unnamed x8 -> x2, local copies, waits for them, and re-layouts: 10.7 us -> 0.01 us
    pallas_call x0 -> x1, Pallas kernels: none -> 2.2 us  [local(): pl.pallas_call(finish, out_shape=(jax.ShapeDtypeStruct((toks, width), BF1...]
where the time goes in v2:
time: 108 us
  Pallas kernels  107 us (99%)
    pallas_call x1, Pallas kernels, local(): pl.pallas_call(functools.partial(kernel, order, plane, min(256, ff // 2))...  105 us
    pallas_call x1, Pallas kernels, local(): pl.pallas_call(finish, out_shape=(jax.ShapeDtypeStruct((toks, width), BF1...  2.2 us

profile of v2, /device:TPU:1, one launch (start us, length us, event | category | flops | bytes accessed | tf_op | source)
XLA Modules:
  0.0 107.7 jit_solution(2767847351843308115)
XLA Ops:
  0.6 0.0 copy-start
  0.6 104.8 %shard_map.102 = (f32[384,1024]{1,0:T(8,128)S(1)}, bf16[128,1024]{1,0:T(8,128)(2,1)S(1)}, bf16[128,1024]{1,0:T(8,128)(2,1)S(1)}, f32[128,1024]{1,0:T(8,128)S(1)}...) custom-call(bf16[128,1024]{1,0:T(8,128)(2,1)} %tokens_hbm.1, ...), custom_call_target="tpu_custom_call" | custom-call | tf_op jit(solution)/shard_map/pallas_call | solution.py:396
  105.4 0.0 copy-done
  105.5 2.2 %shard_map.103 = (bf16[128,1024]{1,0:T(8,128)(2,1)}, bf16[128,1024]{1,0:T(8,128)(2,1)}, bf16[1024,1024]{1,0:T(8,128)(2,1)}, bf16[1024,1024]{1,0:T(8,128)(2,1)}) custom-call(f32[384,1024]{1,0:T(8,128)S(1)} %get-tuple-element.16.total, bf16[128,1024]{1,0:T(8,128)(2,1)S(1)} %get-tuple-element.17.tokens_ref, bf16[128,1024]{1,0:T(8,128)(2,1)S(1)} %get-tuple-element.18.cot_ref, ...), custom_call_target="tpu_custom_call" | custom-call | tf_op jit(solution)/shard_map/pallas_call | solution.py:446
Async XLA Ops:
  0.6 104.8 %copy-start = (f32[1024]{0:T(1024)S(1)}, f32[1024]{0:T(1024)}, u32[]{:S(2)}) copy-start(f32[1024]{0:T(1024)} %param.8) | copy-start | bytes 12292

commit v3 on v2

--- a/solution.py
+++ b/solution.py
@@ -16,9 +16,15 @@
 UNIT = 2 * CAP
 REPS = 4
 PLANE = 8
-ORDERS = {8: (0, 1, 2, 6, 3, 5, 4, 7), 4: (0, 1, 2, 3), 2: (0, 1)}
+ORDERS = {8: (0, 1, 6, 2, 5, 3, 4, 7), 4: (0, 1, 2, 3)}
+FIRST = (0, -1)
+LATE = (0, 1)
 ROOT = math.sqrt(2.0 / math.pi)
 CUBIC = 0.044715
+
+
+def places_of(which, steps):
+    return tuple(i % steps for i in which)
 
 
 def dot(left, right, contract=((1,), (0,))):
@@ -31,8 +37,9 @@
     total, tokens_ref, cot_ref, xhat, scale, columns, g_first, g_second,
     w_first, w_second, sent, landed, gathered, x_rows, d_rows, hidden, d_pre,
     partial, relay, arrived, back, returned, disp, take, rows_in,
+    early, spread_in, late_out, home, home_relay, home_in,
     load_sem, disp_send, disp_recv, ag_send, ag_recv, fw_send, fw_recv,
-    r1_send, r1_recv, r2_send, r2_recv, ret_send, ret_recv,
+    r1_send, r1_recv, r2_send, r2_recv, ret_send, ret_recv, sp_send, sp_recv, lt_send, lt_recv,
 ):
     steps = len(order)
     toks, width = tokens_ref.shape
@@ -40,6 +47,8 @@
     both = 2 * group
     chunk = 2 * REPS * group
     chunks = steps // 2
+    first = places_of(FIRST, steps)
+    lates = places_of(LATE, steps)
     places = steps * plane * UNIT
     me_y = lax.axis_index("rep")
     me_e = lax.axis_index("exp")
@@ -127,10 +136,21 @@
 
     def dispatch(i):
         piece = dot(disp[i * rows_at:(i + 1) * rows_at, :], rows_in[...])
-        sent[i] = piece.reshape(plane, UNIT, width).astype(BF16)
+        piece = piece.reshape(plane, UNIT, width).astype(BF16)
+        if i in first:
+            early[first.index(i), 0] = piece
+        else:
+            sent[i] = piece
         if i == 0:
             pl.semaphore_wait(barrier, experts - 1 + 2)
         away = order[i]
+        if i in first:
+            f = first.index(i)
+            for s, slot in ((0, 1), (1, 3)):
+                remote(early.at[f, 0], early.at[f, slot], ag_send.at[s], ag_recv.at[s, i], sides[s]).start()
+            if i == 0:
+                spread(i, 0)
+            return
         if away == 0:
             pltpu.make_async_copy(sent.at[i, me_p], landed.at[i, me_p], disp_recv.at[i]).start()
 
@@ -169,6 +189,45 @@
         for s, slot in ((0, 1), (1, 3)):
             remote(gathered.at[0, i], gathered.at[slot, i], ag_send.at[s], ag_recv.at[s, i], sides[s]).start()
 
+    def fan(src, dst, send, recv, away):
+        if away == 0:
+            pltpu.make_async_copy(src.at[me_p], dst.at[me_p], recv).start()
+
+        @pl.loop(1 if away == 0 else 0, plane)
+        def _(s):
+            p = lax.rem(me_p + s, plane)
+            remote(src.at[p], dst.at[me_p], send, recv, peer(away, p)).start()
+
+    def spread(i, slot):
+        f = first.index(i)
+        fan(early.at[f, slot], spread_in.at[f, slot], sp_send.at[f, slot], sp_recv.at[f, slot], order[i])
+
+    def forward_early(i):
+        f = first.index(i)
+        for s, slot in ((0, 1), (1, 3)):
+            whole(early.at[f, slot], ag_recv.at[s, i])
+            half = pl.ds(s * (plane // 2), plane // 2)
+            remote(
+                early.at[f, slot, half], early.at[f, 2, half], fw_send.at[s], fw_recv.at[s, i], sides[s]
+            ).start()
+        if i == 0:
+            for slot in (1, 3):
+                spread(i, slot)
+
+    def complete_early(i):
+        f = first.index(i)
+        for s in range(2):
+            whole(early.at[f, 2, pl.ds(s * (plane // 2), plane // 2)], fw_recv.at[s, i])
+        for slot in ((2,) if i == 0 else (0, 1, 3, 2)):
+            spread(i, slot)
+
+    def landed_early(i):
+        f = first.index(i)
+        for slot in (0, 1, 3, 2):
+            whole(spread_in.at[f, slot], sp_recv.at[f, slot])
+            units = spread_in[f, slot].astype(F32).reshape(both, width).astype(BF16)
+            gathered[slot, i] = dot(split_perm(), units).astype(BF16)
+
     def forward(i):
         for s, slot in ((0, 1), (1, 3)):
             whole(gathered.at[slot, i], ag_recv.at[s, i])
@@ -178,6 +237,9 @@
             ).start()
 
     def complete(i):
+        if i in first:
+            landed_early(i)
+            return
         for s in range(2):
             whole(gathered.at[2, i, pl.ds(s * group, group)], fw_recv.at[s, i])
 
@@ -259,13 +321,54 @@
                 back.at[i, p], returned.at[i, me_p], ret_send.at[i], ret_recv.at[i], peer(-away, p)
             ).start()
 
-    def combine(n):
+    def late_send(i):
+        l = lates.index(i)
+        for slot in (2, 3, 1, 0):
+            late_out[l, slot] = dot(merge_perm(), partial[slot, i]).reshape(plane, UNIT, width).astype(BF16)
+            fan(late_out.at[l, slot], home.at[l, slot], lt_send.at[l, slot], lt_recv.at[l, slot], -order[i])
+
+    def late_first(i):
+        l = lates.index(i)
+        whole(home.at[l, 2], lt_recv.at[l, 2])
+        for s in range(2):
+            half = pl.ds(s * (plane // 2), plane // 2)
+            remote(home.at[l, 2, half], home_relay.at[l, s], r1_send.at[s], r1_recv.at[s, i], sides[s]).start()
+        for s in range(2):
+            whole(home.at[l, opposite[s]], lt_recv.at[l, opposite[s]])
+            half = pl.ds((1 - s) * (plane // 2), plane // 2)
+            remote(
+                home.at[l, opposite[s], half], home_in.at[l, s, half], r2_send.at[s], r2_recv.at[s, i], sides[s]
+            ).start()
+
+    def late_second(i):
+        l = lates.index(i)
+        for s in range(2):
+            half = pl.ds(s * (plane // 2), plane // 2)
+            whole(home_relay.at[l, s], r1_recv.at[s, i])
+            summed = home[l, opposite[s], half].astype(F32) + home_relay[l, s].astype(F32)
+            home[l, opposite[s], half] = summed.astype(BF16)
+            remote(
+                home.at[l, opposite[s], half], home_in.at[l, s, half], r2_send.at[s], r2_recv.at[s, i], sides[s]
+            ).start()
+
+    def late_third(i):
+        l = lates.index(i)
+        whole(home.at[l, 0], lt_recv.at[l, 0])
+        for s in range(2):
+            whole(home_in.at[l, s], r2_recv.at[s, i])
+        summed = home[l, 0].astype(F32) + home_in[l, 0].astype(F32) + home_in[l, 1].astype(F32)
+        returned[i] = summed.astype(BF16)
+
+    def combine(n, start):
         for b in range(2):
+            if 2 * n + b in lates:
+                late_third(2 * n + b)
+                continue
             whole(returned.at[2 * n + b], ret_recv.at[2 * n + b])
         span = 2 * rows_at
         units = returned[2 * n:2 * n + 2].astype(F32).reshape(span, width).astype(BF16)
         got = dot(take[:, n * span:(n + 1) * span], units)
-        if n == 0:
+        if start:
             total[...] = got
         else:
             total[...] += got
@@ -284,8 +387,9 @@
 
     tiles = ff // tile
     cut = tiles // 2
-    ready = iter(range(steps))
-    passed = iter(range(steps))
+    normal = [i for i in range(steps) if i not in first]
+    ready = iter(normal)
+    passed = iter(normal)
 
     def arrive_next():
         i = next(ready, None)
@@ -297,57 +401,78 @@
         if i is not None:
             forward(i)
 
-    early = min(4, steps)
-    dispatch(0)
-    dispatch(1)
-    arrive_next()
-    for i in range(2, early):
+    for i in first:
+        dispatch(i)
+    for i in normal[:4]:
+        dispatch(i)
+    write_take()
+    forward_early(0)
+    for i in normal[4:]:
         dispatch(i)
     arrive_next()
-    for i in range(early, steps):
-        dispatch(i)
+    for i in first[1:]:
+        forward_early(i)
+    complete_early(0)
+    arrive_next()
     forward_next()
     arrive_next()
-    write_take()
-    forward_next()
-    arrive_next()
+    for i in first[1:]:
+        complete_early(i)
     loads[2].wait()
     loads[3].wait()
     for n in range(chunks):
+        pair = (2 * n, 2 * n + 1)
+        late = [i for i in pair if i in lates]
+        soon = [i for i in pair if i not in lates]
+        before = [i for i in (2 * n - 2, 2 * n - 1) if i >= 0 and i not in lates]
+        if n == 0:
+            forward_next()
         complete(2 * n)
         complete(2 * n + 1)
         pack(n)
         first_half(n, 0, cut)
+        arrive_next()
+        for i in before[:1]:
+            reduce_second(i)
+        first_half(n, cut, tiles)
         forward_next()
-        if n:
-            reduce_second(2 * n - 2)
-        first_half(n, cut, tiles)
-        arrive_next()
-        forward_next()
-        if n:
-            reduce_second(2 * n - 1)
+        for i in before[1:]:
+            reduce_second(i)
         second_half(n, 0, cut)
         arrive_next()
         second_half(n, cut, tiles)
-        reduce_first((2 * n, 2 * n + 1))
-        if n:
-            give_back(2 * n - 2)
-            give_back(2 * n - 1)
-    n = chunks - 1
-    out_grad(0, cut)
-    reduce_second(2 * n)
+        reduce_first(soon)
+        for i in late:
+            late_send(i)
+        forward_next()
+        if n == chunks - 1:
+            out_grad(0, cut)
+        for i in before:
+            give_back(i)
     out_grad(cut, tiles)
-    reduce_second(2 * n + 1)
+    for i in (steps - 2, steps - 1):
+        reduce_second(i)
+    for i in lates:
+        late_first(i)
     in_grad(0, cut)
-    give_back(2 * n)
+    for i in (steps - 2, steps - 1):
+        give_back(i)
+    for i in lates:
+        late_second(i)
     in_grad(cut, tiles)
-    give_back(2 * n + 1)
-    for n in range(chunks):
-        combine(n)
+    finals = sorted(range(chunks), key=lambda n: (2 * n in lates or 2 * n + 1 in lates, n))
+    for n in finals:
+        combine(n, n == finals[0])
 
     for i in range(steps):
-        for buf, sem in ((sent, disp_send), (back, ret_send)):
+        for buf, sem, other in ((sent, disp_send, first), (back, ret_send, lates)):
+            if i in other:
+                continue
             whole(buf.at[i, 0:plane - 1] if order[i] == 0 else buf.at[i], sem.at[i])
+    for buf, sem, which in ((early, sp_send, first), (late_out, lt_send, lates)):
+        for j, i in enumerate(which):
+            for slot in range(REPS):
+                whole(buf.at[j, slot, 0:plane - 1] if order[i] == 0 else buf.at[j, slot], sem.at[j, slot])
     for s in range(2):
         whole(gathered.at[0], ag_send.at[s])
         whole(gathered.at[0, :, pl.ds(0, group)], fw_send.at[s])
@@ -425,6 +550,12 @@
             pltpu.VMEM((places, 3 * toks), BF16),
             pltpu.VMEM((3 * toks, places), BF16),
             pltpu.VMEM((3 * toks, width), BF16),
+            pltpu.VMEM((len(FIRST), REPS) + unit[1:], BF16),
+            pltpu.VMEM((len(FIRST), REPS) + unit[1:], BF16),
+            pltpu.VMEM((len(LATE), REPS) + unit[1:], BF16),
+            pltpu.VMEM((len(LATE), REPS) + unit[1:], BF16),
+            pltpu.VMEM((len(LATE), 2, plane // 2, UNIT, width), BF16),
+            pltpu.VMEM((len(LATE), 2) + unit[1:], BF16),
             dma((4,)),
             dma((steps,)),
             dma((steps,)),
@@ -438,6 +569,10 @@
             dma((2, steps)),
             dma((steps,)),
             dma((steps,)),
+            dma((len(FIRST), REPS)),
+            dma((len(FIRST), REPS)),
+            dma((len(LATE), REPS)),
+            dma((len(LATE), REPS)),
         ],
         compiler_params=pltpu.CompilerParams(
             collective_id=0, has_side_effects=True, vmem_limit_bytes=53 * 1024 * 1024

time: 108 us -> 90.1 us (0.83)
  Pallas kernels: 107 us -> 89.2 us
    pallas_call x1, Pallas kernels: 105 us -> 87 us  [local(): pl.pallas_call(functools.partial(kernel, order, plane, min(256, ff // 2))...]
where the time goes in v3:
time: 90.1 us; the launch traced here: 90 us
  Pallas kernels  89.2 us (99%)
    pallas_call x1, Pallas kernels, local(): pl.pallas_call(functools.partial(kernel, order, plane, min(256, ff // 2))...  87 us
    pallas_call x1, Pallas kernels, local(): pl.pallas_call(finish, out_shape=(jax.ShapeDtypeStruct((toks, width), BF1...  2.2 us

profile of v3, /device:TPU:1, one launch (start us, length us, event | category | flops | bytes accessed | tf_op | source)
XLA Modules:
  0.0 90.0 jit_solution(15443853335237250169)
XLA Ops:
  0.6 0.0 copy-start
  0.6 87.0 %shard_map.102 = (f32[384,1024]{1,0:T(8,128)S(1)}, bf16[128,1024]{1,0:T(8,128)(2,1)S(1)}, bf16[128,1024]{1,0:T(8,128)(2,1)S(1)}, f32[128,1024]{1,0:T(8,128)S(1)}...) custom-call(bf16[128,1024]{1,0:T(8,128)(2,1)} %tokens_hbm.1, ...), custom_call_target="tpu_custom_call" | custom-call | tf_op jit(solution)/shard_map/pallas_call | solution.py:521
  87.6 0.0 copy-done
  87.7 2.2 %shard_map.103 = (bf16[128,1024]{1,0:T(8,128)(2,1)}, bf16[128,1024]{1,0:T(8,128)(2,1)}, bf16[1024,1024]{1,0:T(8,128)(2,1)}, bf16[1024,1024]{1,0:T(8,128)(2,1)}) custom-call(f32[384,1024]{1,0:T(8,128)S(1)} %get-tuple-element.16.total, bf16[128,1024]{1,0:T(8,128)(2,1)S(1)} %get-tuple-element.17.tokens_ref, bf16[128,1024]{1,0:T(8,128)(2,1)S(1)} %get-tuple-element.18.cot_ref, ...), custom_call_target="tpu_custom_call" | custom-call | tf_op jit(solution)/shard_map/pallas_call | solution.py:581
Async XLA Ops:
  0.6 87.0 %copy-start = (f32[1024]{0:T(1024)S(1)}, f32[1024]{0:T(1024)}, u32[]{:S(2)}) copy-start(f32[1024]{0:T(1024)} %param.8) | copy-start | bytes 12292

commit v4 on v3

--- a/solution.py
+++ b/solution.py
@@ -33,11 +33,11 @@
 
 def kernel(
     order, plane, tile,
-    tokens_hbm, gain_ref, ids_ref, gates_ref, cot_hbm, w_in_ref, w_out_ref,
+    tokens_hbm, gain_hbm, ids_hbm, gates_hbm, cot_hbm, w_in_ref, w_out_ref,
     total, tokens_ref, cot_ref, xhat, scale, columns, g_first, g_second,
     w_first, w_second, sent, landed, gathered, x_rows, d_rows, hidden, d_pre,
     partial, relay, arrived, back, returned, disp, take, rows_in,
-    early, spread_in, late_out, home, home_relay, home_in,
+    early, spread_in, late_out, home, home_relay, home_in, gain_ref, ids_ref, gates_ref,
     load_sem, disp_send, disp_recv, ag_send, ag_recv, fw_send, fw_recv,
     r1_send, r1_recv, r2_send, r2_recv, ret_send, ret_recv, sp_send, sp_recv, lt_send, lt_recv,
 ):
@@ -62,11 +62,14 @@
     loads = [
         pltpu.make_async_copy(src, dst, load_sem.at[j])
         for j, (src, dst) in enumerate(
-            ((tokens_hbm, tokens_ref), (cot_hbm, cot_ref), (w_in_ref, w_first), (w_out_ref, w_second))
+            (
+                (tokens_hbm, tokens_ref), (cot_hbm, cot_ref), (w_in_ref, w_first), (w_out_ref, w_second),
+                (ids_hbm, ids_ref), (gates_hbm, gates_ref), (gain_hbm, gain_ref),
+            )
         )
     ]
-    loads[0].start()
-    loads[1].start()
+    for j in (4, 5, 0, 1, 6):
+        loads[j].start()
 
     barrier = pltpu.get_barrier_semaphore()
     for side in sides:
@@ -79,6 +82,8 @@
     loads[2].start()
     loads[3].start()
 
+    loads[4].wait()
+    loads[5].wait()
     def place_of(k):
         ids = ids_ref[k:k + 1, :]
         z = lax.rem(lax.div(ids, plane) - me_z + steps, steps)
@@ -108,6 +113,7 @@
         disp[:, (k + 1) * toks:(k + 2) * toks] = (down_q == targets[k] + CAP).astype(F32).astype(BF16)
 
     loads[0].wait()
+    loads[6].wait()
     values = tokens_ref[...].astype(F32)
     center = values - jnp.mean(values, axis=-1, keepdims=True)
     inv = lax.rsqrt(jnp.mean(center * center, axis=-1, keepdims=True) + EPSILON)
@@ -442,13 +448,13 @@
         arrive_next()
         second_half(n, cut, tiles)
         reduce_first(soon)
+        forward_next()
         for i in late:
             late_send(i)
-        forward_next()
+        for i in before:
+            give_back(i)
         if n == chunks - 1:
             out_grad(0, cut)
-        for i in before:
-            give_back(i)
     out_grad(cut, tiles)
     for i in (steps - 2, steps - 1):
         reduce_second(i)
@@ -460,7 +466,7 @@
     for i in lates:
         late_second(i)
     in_grad(cut, tiles)
-    finals = sorted(range(chunks), key=lambda n: (2 * n in lates or 2 * n + 1 in lates, n))
+    finals = list(range(1, chunks - 1)) + [0, chunks - 1]
     for n in finals:
         combine(n, n == finals[0])
 
@@ -530,7 +536,7 @@
             pltpu.VMEM((width, ff), BF16),
             pltpu.VMEM((ff, width), BF16),
         ),
-        in_specs=[hbm, vmem, vmem, vmem, hbm, hbm, hbm],
+        in_specs=[hbm] * 7,
         out_specs=(vmem,) * 8,
         scratch_shapes=[
             pltpu.VMEM((width, ff), BF16),
@@ -556,7 +562,10 @@
             pltpu.VMEM((len(LATE), REPS) + unit[1:], BF16),
             pltpu.VMEM((len(LATE), 2, plane // 2, UNIT, width), BF16),
             pltpu.VMEM((len(LATE), 2) + unit[1:], BF16),
-            dma((4,)),
+            pltpu.VMEM((1, width), F32),
+            pltpu.VMEM((2, toks), jnp.int32),
+            pltpu.VMEM((2, toks), F32),
+            dma((7,)),
             dma((steps,)),
             dma((steps,)),
             dma((2,)),

time: 90.1 us -> 89.5 us (level)
  no operation moved by 1% of the time
where the time goes in v4:
time: 89.5 us; the launch traced here: 89.4 us
  Pallas kernels  88.6 us (99%)
    pallas_call x1, Pallas kernels, local(): pl.pallas_call(functools.partial(kernel, order, plane, min(256, ff // 2))...  86.4 us
    pallas_call x1, Pallas kernels, local(): pl.pallas_call(finish, out_shape=(jax.ShapeDtypeStruct((toks, width), BF1...  2.2 us

profile of v4, /device:TPU:1, one launch (start us, length us, event | category | flops | bytes accessed | tf_op | source)
XLA Modules:
  0.0 89.4 jit_solution(10760360445504377726)
XLA Ops:
  0.6 0.0 copy-start
  0.6 86.4 %shard_map.102 = (f32[384,1024]{1,0:T(8,128)S(1)}, bf16[128,1024]{1,0:T(8,128)(2,1)S(1)}, bf16[128,1024]{1,0:T(8,128)(2,1)S(1)}, f32[128,1024]{1,0:T(8,128)S(1)}...) custom-call(bf16[128,1024]{1,0:T(8,128)(2,1)} %tokens_hbm.1, ...), custom_call_target="tpu_custom_call" | custom-call | tf_op jit(solution)/shard_map/pallas_call | solution.py:527
  87.1 0.0 copy-done
  87.1 2.2 %shard_map.103 = (bf16[128,1024]{1,0:T(8,128)(2,1)}, bf16[128,1024]{1,0:T(8,128)(2,1)}, bf16[1024,1024]{1,0:T(8,128)(2,1)}, bf16[1024,1024]{1,0:T(8,128)(2,1)}) custom-call(f32[384,1024]{1,0:T(8,128)S(1)} %get-tuple-element.16.total, bf16[128,1024]{1,0:T(8,128)(2,1)S(1)} %get-tuple-element.17.tokens_ref, bf16[128,1024]{1,0:T(8,128)(2,1)S(1)} %get-tuple-element.18.cot_ref, ...), custom_call_target="tpu_custom_call" | custom-call | tf_op jit(solution)/shard_map/pallas_call | solution.py:590
Async XLA Ops:
  0.6 86.4 %copy-start = (f32[1024]{0:T(1024)S(1)}, f32[1024]{0:T(1024)}, u32[]{:S(2)}) copy-start(f32[1024]{0:T(1024)} %param.8) | copy-start | bytes 12292

commit v5 on v4

--- a/solution.py
+++ b/solution.py
@@ -407,9 +407,11 @@
         if i is not None:
             forward(i)
 
-    for i in first:
+    dispatch(0)
+    dispatch(normal[0])
+    for i in first[1:]:
         dispatch(i)
-    for i in normal[:4]:
+    for i in normal[1:4]:
         dispatch(i)
     write_take()
     forward_early(0)

time: 89.5 us -> 89.4 us (level)
  no operation moved by 1% of the time
where the time goes in v5:
time: 89.4 us; the launch traced here: 89.3 us
  Pallas kernels  88.5 us (99%)
    pallas_call x1, Pallas kernels, local(): pl.pallas_call(functools.partial(kernel, order, plane, min(256, ff // 2))...  86.3 us
    pallas_call x1, Pallas kernels, local(): pl.pallas_call(finish, out_shape=(jax.ShapeDtypeStruct((toks, width), BF1...  2.2 us

profile of v5, /device:TPU:1, one launch (start us, length us, event | category | flops | bytes accessed | tf_op | source)
XLA Modules:
  0.0 89.3 jit_solution(1341260443128052524)
XLA Ops:
  0.6 0.0 copy-start
  0.6 86.3 %shard_map.102 = (f32[384,1024]{1,0:T(8,128)S(1)}, bf16[128,1024]{1,0:T(8,128)(2,1)S(1)}, bf16[128,1024]{1,0:T(8,128)(2,1)S(1)}, f32[128,1024]{1,0:T(8,128)S(1)}...) custom-call(bf16[128,1024]{1,0:T(8,128)(2,1)} %tokens_hbm.1, ...), custom_call_target="tpu_custom_call" | custom-call | tf_op jit(solution)/shard_map/pallas_call | solution.py:529
  86.9 0.0 copy-done
  86.9 2.2 %shard_map.103 = (bf16[128,1024]{1,0:T(8,128)(2,1)}, bf16[128,1024]{1,0:T(8,128)(2,1)}, bf16[1024,1024]{1,0:T(8,128)(2,1)}, bf16[1024,1024]{1,0:T(8,128)(2,1)}) custom-call(f32[384,1024]{1,0:T(8,128)S(1)} %get-tuple-element.16.total, bf16[128,1024]{1,0:T(8,128)(2,1)S(1)} %get-tuple-element.17.tokens_ref, bf16[128,1024]{1,0:T(8,128)(2,1)S(1)} %get-tuple-element.18.cot_ref, ...), custom_call_target="tpu_custom_call" | custom-call | tf_op jit(solution)/shard_map/pallas_call | solution.py:592
Async XLA Ops:
  0.6 86.3 %copy-start = (f32[1024]{0:T(1024)S(1)}, f32[1024]{0:T(1024)}, u32[]{:S(2)}) copy-start(f32[1024]{0:T(1024)} %param.8) | copy-start | bytes 12292
